TPU v7x, 256 devices: a whole 4x4x8 slice. The times are simulated.
256 devices in a mesh: seq: 32 (over z, x), vocab: 8 (over y, core).
Axes of the slice: x: 4, y: 4, z: 8, core: 2. Of those that a mesh axis runs over, the one named last changes fastest.
Arguments:
- hidden: bfloat16 [512, 5120], P(('seq', 'vocab')), may hold values from -400 to 400
- norm_gain: float32 [5120], replicated, may hold values from 0.1 to 1.9
- head_weight: bfloat16 [5120, 131072], P(None, ('seq', 'vocab')), may hold values from -2 to 2
- teacher_logits: bfloat16 [1024, 32, 4096], P('seq', None, 'vocab'), may hold values from -12 to 300
- teacher_slot: int32 [512], replicated, may hold values from 0 to 1023, as said below
- valid_tokens: int32 [512], replicated, may hold values 0 or 1
Outputs:
- grad_hidden: bfloat16 [512, 5120], P(('seq', 'vocab'))
- grad_head: bfloat16 [5120, 131072], P(None, ('seq', 'vocab'))
Inputs may be any that keep to these rules, and one draw needn't show every extreme that they name: `teacher_slot`: rows use distinct slots; slots g * 32 to (g + 1) * 32 - 1 belong to sequence group g of the teacher's packing; at most 32 rows use one group's slots, and some group holds 32 in every draw.
All inputs are finite; a program needn't handle non-finite values.
Results may differ from a plain program's by a relative error of at most 0.02.
Values may be sent and summed in bfloat16 or wider, within the bound.
A program may use at most 128 MiB of HBM per device.

v0:
```python
import jax
import jax.numpy as jnp
from jax import lax
from jax.sharding import PartitionSpec as P

epsilon = 1e-06


def shards(hidden, norm_gain, head_weight, teacher_logits, teacher_slot, valid_tokens):
    widened = hidden.astype(jnp.float32)
    inv_rms = lax.rsqrt(jnp.mean(widened * widened, axis=1, keepdims=True) + epsilon)
    normed = widened * inv_rms
    features = (normed * norm_gain).astype(jnp.bfloat16)
    gathered = lax.all_gather(features, ("seq", "vocab"), axis=0, tiled=True)
    logits = jnp.dot(gathered, head_weight, preferred_element_type=jnp.float32)
    arrived = lax.all_to_all(teacher_logits, "seq", split_axis=1, concat_axis=0, tiled=True)
    slot_table = arrived.reshape(arrived.shape[0], arrived.shape[2])
    teacher = jnp.take(slot_table, teacher_slot, axis=0).astype(jnp.float32)
    student_top, teacher_top = lax.pmax(
        (jnp.max(logits, axis=1), jnp.max(teacher, axis=1)), ("seq", "vocab")
    )
    shifted = jnp.exp(logits - student_top[:, None])
    teacher_shifted = jnp.exp(teacher - teacher_top[:, None])
    student_total, cross_sum, teacher_total = lax.psum(
        (
            jnp.sum(shifted, axis=1),
            jnp.sum(shifted * (logits - teacher), axis=1),
            jnp.sum(teacher_shifted, axis=1),
        ),
        ("seq", "vocab"),
    )
    student_lse = (student_top + jnp.log(student_total))[:, None]
    teacher_lse = (teacher_top + jnp.log(teacher_total))[:, None]
    divergence = cross_sum[:, None] / student_total[:, None] - student_lse + teacher_lse
    student_prob = jnp.exp(logits - student_lse)
    log_gap = logits - student_lse - (teacher - teacher_lse)
    row_weight = valid_tokens.astype(jnp.float32)[:, None]
    logit_grad = (row_weight * student_prob * (log_gap - divergence)).astype(jnp.bfloat16)
    grad_head = lax.dot_general(
        gathered, logit_grad, (((0,), (0,)), ((), ())), preferred_element_type=jnp.float32
    ).astype(jnp.bfloat16)
    feature_grad = lax.psum_scatter(
        lax.dot_general(
            logit_grad, head_weight, (((1,), (1,)), ((), ())), preferred_element_type=jnp.float32
        ),
        ("seq", "vocab"),
        scatter_dimension=0,
        tiled=True,
    )
    norm_grad = feature_grad * norm_gain
    grad_hidden = inv_rms * (
        norm_grad - normed * jnp.mean(norm_grad * normed, axis=1, keepdims=True)
    )
    return (grad_hidden.astype(jnp.bfloat16), grad_head)


def solution(mesh):
    placed = (
        P(("seq", "vocab"), None),
        P(),
        P(None, ("seq", "vocab")),
        P("seq", None, "vocab"),
        P(),
        P(),
    )
    return jax.shard_map(
        shards,
        mesh=mesh,
        in_specs=placed,
        out_specs=(P(("seq", "vocab"), None), P(None, ("seq", "vocab"))),
        check_vma=False,
    )
```

profile of v0, /device:TPU:97, one launch (start us, length us, event | category | flops | bytes accessed | tf_op | source)
XLA Modules:
  0.0 599.2 jit_solution(9775091275247822466)
XLA Ops:
  7.2 0.0 all-gather.3.cloned.1.call-start
  7.2 0.9 fusion.17
  8.1 1.4 fusion.19
  9.5 0.0 all-gather.3.cloned.1.call-update
  9.6 2.8 copy.10
  12.3 9.7 %all-to-all-start = ((bf16[32,32,512]{2,0,1:T(8,128)(2,1)}), bf16[32,32,512]{2,0,1:T(8,128)(2,1)S(1)}, u32[]{:S(2)}, u32[]{:S(2)}) async-start(bf16[32,32,512]{2,0,1:T(8,128)(2,1)} %copy.10), calls=%async_computation | async-start | bytes 2097152 | tf_op jit(solution)/shard_map/all_to_all | solution.py:16
  22.1 0.0 all-reduce.5.cloned.1.call-start
  22.1 0.7 convert_element_type.22
  22.8 0.7 compare_select_fusion
  23.5 0.7 compare_and_fusion
  24.2 23.7 %all-to-all-done = bf16[32,32,512]{2,0,1:T(8,128)(2,1)S(1)} async-done(((bf16[32,32,512]{2,0,1:T(8,128)(2,1)}), bf16[32,32,512]{2,0,1:T(8,128)(2,1)S(1)}, u32[]{:S(2)}, u32[]{:S(2)}) %all-to-all-start) | async-done | bytes 1048608 | tf_op jit(solution)/shard_map/all_to_all | solution.py:16
  47.9 2.0 gather_fusion
  49.8 0.2 copy.11
  50.1 0.2 fusion.9
  50.2 80.9 %all-gather.3.cloned.1.call-done = bf16[256,2,5120]{2,1,0:T(2,128)(2,1)} async-done(((bf16[1,2,5120]{2,1,0:T(2,128)(2,1)}), bf16[256,2,5120]{2,1,0:T(2,128)(2,1)}) %all-gather.3.cloned.1.call-update) | async-done | bytes 5242896 | tf_op jit(solution)/shard_map/all_gather | solution.py:14
  131.1 11.5 %reshape.46 = bf16[512,5120]{1,0:T(8,128)(2,1)} reshape(bf16[256,2,5120]{2,1,0:T(2,128)(2,1)} %all-gather.3.cloned.1.call-done) | data formatting | bytes 10485760
  142.6 7.2 %fusion.20 = (f32[512]{0:T(512)S(1)}, f32[512,512]{0,1:T(8,128)S(1)}) fusion(bf16[512,5120]{1,0:T(8,128)(2,1)} %reshape.46, bf16[5120,512]{1,0:T(8,128)(2,1)} %param.8), kind=kOutput, calls=%fused_computation.38 | convolution fusion | flops 2684616192 | bytes 11536384 | tf_op jit(solution)/shard_map/dot_general | solution.py:15
  149.8 74.6 %all-reduce.2 = (f32[512]{0:T(512)S(1)}, f32[512]{0:T(512)S(1)}) all-reduce(bf16[512]{0:T(512)(128)(2,1)S(1)} %fusion.9, f32[512]{0:T(512)S(1)} %get-tuple-element.13), channel_id=1, replica_groups=mesh['seq'=32,'vocab'=8] {'seq','vocab'}, use_global_device_ids=true, to_apply=%region_6.7 | all-reduce | flops 1024 | bytes 7168 | tf_op jit(solution)/shard_map/pmax | solution.py:19
  224.4 0.5 fusion.8
  224.9 74.2 %all-reduce.1 = (f32[512]{0:T(512)S(1)}, f32[512]{0:T(512)S(1)}, f32[512]{0:T(512)S(1)}) all-reduce(f32[512]{0:T(512)S(1)} %get-tuple-element.4, f32[512]{0:T(512)S(1)} %get-tuple-element.3, f32[512]{0:T(512)S(1)} %get-tuple-element.2), channel_id=1, replica_groups=mesh['seq'=32,'vocab'=8] {'seq','vocab'}, use_global_device_ids=true, to_apply=%region_8.9 | all-reduce | flops 1536 | bytes 12288 | tf_op jit(solution)/shard_map/psum | solution.py:24
  299.1 0.4 fusion.5
  299.5 8.0 %fusion.21 = f32[512,5120]{1,0:T(8,128)} fusion(bf16[512,512]{0,1:T(8,128)(2,1)S(1)} %fusion.5, bf16[5120,512]{1,0:T(8,128)(2,1)} %param.8), kind=kOutput, calls=%fused_computation.39 | convolution fusion | flops 2684354560 | bytes 16252928 | tf_op jit(solution)/shard_map/dot_general | solution.py:43
  307.5 0.0 all-reduce.5.cloned.1.call-update
  307.5 0.0 copy-start
  307.5 0.0 copy-start.1
  307.5 7.2 %convolution_convert_fusion = bf16[5120,512]{1,0:T(8,128)(2,1)} fusion(bf16[512,5120]{1,0:T(8,128)(2,1)} %reshape.46, bf16[512,512]{0,1:T(8,128)(2,1)S(1)} %fusion.5), kind=kOutput, calls=%fused_computation.1 | convolution fusion | flops 2686976000 | bytes 11010048 | tf_op jit(solution)/shard_map/dot_general | solution.py:39
  314.7 274.8 %all-reduce.5.cloned.1.call-done = f32[512,5120]{1,0:T(8,128)} async-done(((f32[512,5120]{1,0:T(8,128)}), f32[512,5120]{1,0:T(8,128)}) %all-reduce.5.cloned.1.call-update) | async-done | bytes 10485776
  589.5 0.0 copy-done
  589.5 0.0 copy-done.1
  589.5 1.1 fusion.14
  590.7 1.6 fusion.18
  (4 shorter events, 0.0 us)
Async XLA Ops:
  7.2 124.0 %all-gather.3.cloned.1.call-start = ((), (), s32[]{:S(2)}) async-start(), calls=%async_computation.1 | async-start | bytes 5263360 | tf_op jit(solution)/shard_map/all_gather | solution.py:14
  12.3 35.5 %all-to-all-start = ((bf16[32,32,512]{2,0,1:T(8,128)(2,1)}), bf16[32,32,512]{2,0,1:T(8,128)(2,1)S(1)}, u32[]{:S(2)}, u32[]{:S(2)}) async-start(bf16[32,32,512]{2,0,1:T(8,128)(2,1)} %copy.10), calls=%async_computation | async-start | bytes 2097152 | tf_op jit(solution)/shard_map/all_to_all | solution.py:16
  22.1 567.5 %all-reduce.5.cloned.1.call-start = ((), (), s32[]{:S(2)}) async-start(), calls=%async_computation.2 | async-start | bytes 20971520
  307.5 282.0 %copy-start = (bf16[2,5120]{1,0:T(2,128)(2,1)S(1)}, bf16[2,5120]{1,0:T(2,128)(2,1)}, u32[]{:S(2)}) copy-start(bf16[2,5120]{1,0:T(2,128)(2,1)} %param.6) | copy-start | bytes 61444
  307.5 282.0 %copy-start.1 = (f32[5120]{0:T(1024)S(1)}, f32[5120]{0:T(1024)}, u32[]{:S(2)}) copy-start(f32[5120]{0:T(1024)} %param.7) | copy-start | bytes 61444
Sparse Core Ops, SparseCore 0:
  12.3 118.8 all-gather.2
  307.6 281.8 all-reduce.4
where the time goes:
time: 600 us; the launch traced here: 599 us
  waiting for transfers between devices  379 us (63%)
  blocking collectives  149 us (25%)
  matrix products  22.3 us (4%)
  local copies, waits for them, and re-layouts  16.4 us (3%)
  between operations  14.1 us (2%)
  starting transfers between devices  9.8 us (2%)
  other arithmetic  8.17 us (1%)
    unnamed x3, waiting for transfers between devices  275 us
    all_gather x1, waiting for transfers between devices, shards(): gathered = lax.all_gather(features, ('seq', 'vocab'), axis=0, tiled=True)  80.9 us
    pmax x1, blocking collectives, shards(): lax.pmax((jnp.max(logits, axis=1), jnp.max(teacher, axis=1)), ('seq', 'vo...  74.6 us
    psum x1, blocking collectives, shards(): lax.psum((jnp.sum(shifted, axis=1), jnp.sum(shifted * (logits - teacher),...  74.2 us
    all_to_all x1, waiting for transfers between devices, shards(): lax.all_to_all(teacher_logits, 'seq', split_axis=1, concat_axis=0, tiled=...  23.7 us
    unnamed x6, local copies, waits for them, and re-layouts  14.2 us
  transfers between devices with their start and end apart: 3, of which 3 were waited for; matrix products, arithmetic and copies ran while one was open for 2% of the time, Pallas kernels for 0%

commit v1 on v0

--- a/solution.py
+++ b/solution.py
@@ -11,7 +11,13 @@
     inv_rms = lax.rsqrt(jnp.mean(widened * widened, axis=1, keepdims=True) + epsilon)
     normed = widened * inv_rms
     features = (normed * norm_gain).astype(jnp.bfloat16)
-    gathered = lax.all_gather(features, ("seq", "vocab"), axis=0, tiled=True)
+
+    def _time_series_all(sample):
+        u1 = jnp.stack([sample for _ in range(lax.axis_size(("seq", "vocab")))], 0)
+        side_arr = jnp.concatenate(lax.all_to_all(u1, ("seq", "vocab"), 0, 0), 0)
+        return side_arr
+
+    gathered = _time_series_all(features)
     logits = jnp.dot(gathered, head_weight, preferred_element_type=jnp.float32)
     arrived = lax.all_to_all(teacher_logits, "seq", split_axis=1, concat_axis=0, tiled=True)
     slot_table = arrived.reshape(arrived.shape[0], arrived.shape[2])

time: 600 us -> 649 us (1.082)
  waiting for transfers between devices: 379 us -> 412 us
  starting transfers between devices: 9.8 us -> 23.4 us
    all_to_all x0 -> x1, waiting for transfers between devices: none -> 113 us  [_time_series_all(): side_arr = jnp.concatenate(lax.all_to_all(u1, ('seq', 'vocab'), 0, 0), 0)]
    all_gather x1 -> x0, waiting for transfers between devices: 80.9 us -> none  [shards(): gathered = lax.all_gather(features, ('seq', 'vocab'), axis=0, tiled=True)]
    all_to_all x0 -> x1, starting transfers between devices: none -> 13.6 us  [_time_series_all(): side_arr = jnp.concatenate(lax.all_to_all(u1, ('seq', 'vocab'), 0, 0), 0)]
    reshape x0 -> x1, local copies, waits for them, and re-layouts: none -> 11.5 us  [_time_series_all(): side_arr = jnp.concatenate(lax.all_to_all(u1, ('seq', 'vocab'), 0, 0), 0)]
    unnamed x6 -> x9, local copies, waits for them, and re-layouts: 14.2 us -> 2.79 us
    unnamed x3 -> x2, waiting for transfers between devices: 275 us -> 275 us
where the time goes in v1:
time: 649 us; the launch traced here: 648 us
  waiting for transfers between devices  412 us (63%)
  blocking collectives  150 us (23%)
  starting transfers between devices  23.4 us (4%)
  matrix products  22.4 us (3%)
  local copies, waits for them, and re-layouts  21.5 us (3%)
  between operations  14.1 us (2%)
    unnamed x2, waiting for transfers between devices  275 us
    all_to_all x1, waiting for transfers between devices, _time_series_all(): side_arr = jnp.concatenate(lax.all_to_all(u1, ('seq', 'vocab'), 0, 0), 0)  113 us
    pmax x1, blocking collectives, shards(): lax.pmax((jnp.max(logits, axis=1), jnp.max(teacher, axis=1)), ('seq', 'vo...  75.6 us
    psum x1, blocking collectives, shards(): lax.psum((jnp.sum(shifted, axis=1), jnp.sum(shifted * (logits - teacher),...  74.1 us
    all_to_all x1, waiting for transfers between devices, shards(): lax.all_to_all(teacher_logits, 'seq', split_axis=1, concat_axis=0, tiled=...  23.8 us
    all_to_all x1, starting transfers between devices, _time_series_all(): side_arr = jnp.concatenate(lax.all_to_all(u1, ('seq', 'vocab'), 0, 0), 0)  13.6 us
  transfers between devices with their start and end apart: 3, of which 3 were waited for; matrix products, arithmetic and copies ran while one was open for 2% of the time, Pallas kernels for 0%

profile of v1, /device:TPU:97, one launch (start us, length us, event | category | flops | bytes accessed | tf_op | source)
XLA Modules:
  0.0 648.2 jit_solution(939039543705293786)
XLA Ops:
  7.2 2.8 copy.10
  9.9 9.7 %all-to-all-start.1 = ((bf16[32,32,512]{2,0,1:T(8,128)(2,1)}), bf16[32,32,512]{2,0,1:T(8,128)(2,1)S(1)}, u32[]{:S(2)}, u32[]{:S(2)}) async-start(bf16[32,32,512]{2,0,1:T(8,128)(2,1)} %copy.10), calls=%async_computation.1 | async-start | bytes 2097152 | tf_op jit(solution)/shard_map/all_to_all | solution.py:22
  19.7 0.9 fusion.17
  20.6 0.8 fusion.13
  21.4 23.8 %all-to-all-done.1 = bf16[32,32,512]{2,0,1:T(8,128)(2,1)S(1)} async-done(((bf16[32,32,512]{2,0,1:T(8,128)(2,1)}), bf16[32,32,512]{2,0,1:T(8,128)(2,1)S(1)}, u32[]{:S(2)}, u32[]{:S(2)}) %all-to-all-start.1) | async-done | bytes 1048608 | tf_op jit(solution)/shard_map/all_to_all | solution.py:22
  45.2 5.1 stack.2
  50.2 0.0 copy-start.3
  50.2 0.0 copy-start.2
  50.2 13.6 %all-to-all-start = ((bf16[256,2,5120]{2,1,0:T(2,128)(2,1)}), bf16[256,2,5120]{2,1,0:T(2,128)(2,1)}, u32[]{:S(2)}, u32[]{:S(2)}) async-start(bf16[256,2,5120]{2,1,0:T(2,128)(2,1)} %stack.2), calls=%async_computation | async-start | bytes 10485760 | tf_op jit(solution)/shard_map/all_to_all | solution.py:17
  63.8 0.0 all-reduce.5.cloned.1.call-start
  63.9 0.0 copy-done.3
  63.9 0.0 copy-done.2
  64.0 2.0 gather_fusion
  65.9 0.2 copy.11
  66.2 0.2 fusion.9
  66.3 112.8 %all-to-all-done = bf16[256,2,5120]{2,1,0:T(2,128)(2,1)} async-done(((bf16[256,2,5120]{2,1,0:T(2,128)(2,1)}), bf16[256,2,5120]{2,1,0:T(2,128)(2,1)}, u32[]{:S(2)}, u32[]{:S(2)}) %all-to-all-start) | async-done | bytes 5242912 | tf_op jit(solution)/shard_map/all_to_all | solution.py:17
  179.1 11.5 %reshape.40 = bf16[512,5120]{1,0:T(8,128)(2,1)} reshape(bf16[256,2,5120]{2,1,0:T(2,128)(2,1)} %all-to-all-done) | data formatting | bytes 10485760 | tf_op jit(solution)/shard_map/reshape | solution.py:17
  190.6 7.2 %fusion.19 = (f32[512]{0:T(512)S(1)}, f32[512,512]{0,1:T(8,128)S(1)}) fusion(bf16[512,5120]{1,0:T(8,128)(2,1)} %reshape.40, bf16[5120,512]{1,0:T(8,128)(2,1)} %param.8), kind=kOutput, calls=%fused_computation.37 | convolution fusion | flops 2684616192 | bytes 11536384 | tf_op jit(solution)/shard_map/dot_general | solution.py:21
  197.8 75.6 %all-reduce.2 = (f32[512]{0:T(512)S(1)}, f32[512]{0:T(512)S(1)}) all-reduce(bf16[512]{0:T(512)(128)(2,1)S(1)} %fusion.9, f32[512]{0:T(512)S(1)} %get-tuple-element.13), channel_id=1, replica_groups=mesh['seq'=32,'vocab'=8] {'seq','vocab'}, use_global_device_ids=true, to_apply=%region_6.7 | all-reduce | flops 1024 | bytes 7168 | tf_op jit(solution)/shard_map/pmax | solution.py:25
  273.4 0.5 fusion.8
  273.8 74.1 %all-reduce.1 = (f32[512]{0:T(512)S(1)}, f32[512]{0:T(512)S(1)}, f32[512]{0:T(512)S(1)}) all-reduce(f32[512]{0:T(512)S(1)} %get-tuple-element.4, f32[512]{0:T(512)S(1)} %get-tuple-element.3, f32[512]{0:T(512)S(1)} %get-tuple-element.2), channel_id=1, replica_groups=mesh['seq'=32,'vocab'=8] {'seq','vocab'}, use_global_device_ids=true, to_apply=%region_8.9 | all-reduce | flops 1536 | bytes 12288 | tf_op jit(solution)/shard_map/psum | solution.py:30
  347.9 0.4 fusion.5
  348.3 8.0 %fusion.20 = f32[512,5120]{1,0:T(8,128)} fusion(bf16[512,512]{0,1:T(8,128)(2,1)S(1)} %fusion.5, bf16[5120,512]{1,0:T(8,128)(2,1)} %param.8), kind=kOutput, calls=%fused_computation.38 | convolution fusion | flops 2684354560 | bytes 16252928 | tf_op jit(solution)/shard_map/dot_general | solution.py:49
  356.3 0.0 all-reduce.5.cloned.1.call-update
  356.3 0.0 copy-start
  356.3 0.0 copy-start.1
  356.3 7.2 %convolution_convert_fusion = bf16[5120,512]{1,0:T(8,128)(2,1)} fusion(bf16[512,5120]{1,0:T(8,128)(2,1)} %reshape.40, bf16[512,512]{0,1:T(8,128)(2,1)S(1)} %fusion.5), kind=kOutput, calls=%fused_computation.1 | convolution fusion | flops 2686976000 | bytes 11010048 | tf_op jit(solution)/shard_map/dot_general | solution.py:45
  363.5 275.1 %all-reduce.5.cloned.1.call-done = f32[512,5120]{1,0:T(8,128)} async-done(((f32[512,5120]{1,0:T(8,128)}), f32[512,5120]{1,0:T(8,128)}) %all-reduce.5.cloned.1.call-update) | async-done | bytes 10485776
  638.6 0.0 copy-done
  638.6 0.0 copy-done.1
  638.6 1.1 fusion.14
  639.7 1.6 fusion.18
  (7 shorter events, 0.0 us)
Async XLA Ops:
  9.9 35.2 %all-to-all-start.1 = ((bf16[32,32,512]{2,0,1:T(8,128)(2,1)}), bf16[32,32,512]{2,0,1:T(8,128)(2,1)S(1)}, u32[]{:S(2)}, u32[]{:S(2)}) async-start(bf16[32,32,512]{2,0,1:T(8,128)(2,1)} %copy.10), calls=%async_computation.1 | async-start | bytes 2097152 | tf_op jit(solution)/shard_map/all_to_all | solution.py:22
  50.2 13.7 %copy-start.3 = (s32[512]{0:T(512)S(1)}, s32[512]{0:T(512)}, u32[]{:S(2)}) copy-start(s32[512]{0:T(512)} %param.11) | copy-start | bytes 6148
  50.2 13.7 %copy-start.2 = (s32[512]{0:T(512)S(1)}, s32[512]{0:T(512)}, u32[]{:S(2)}) copy-start(s32[512]{0:T(512)} %param.10) | copy-start | bytes 6148
  50.2 128.9 %all-to-all-start = ((bf16[256,2,5120]{2,1,0:T(2,128)(2,1)}), bf16[256,2,5120]{2,1,0:T(2,128)(2,1)}, u32[]{:S(2)}, u32[]{:S(2)}) async-start(bf16[256,2,5120]{2,1,0:T(2,128)(2,1)} %stack.2), calls=%async_computation | async-start | bytes 10485760 | tf_op jit(solution)/shard_map/all_to_all | solution.py:17
  63.8 574.7 %all-reduce.5.cloned.1.call-start = ((), (), s32[]{:S(2)}) async-start(), calls=%async_computation.2 | async-start | bytes 20971520
  356.3 282.3 %copy-start = (bf16[2,5120]{1,0:T(2,128)(2,1)S(1)}, bf16[2,5120]{1,0:T(2,128)(2,1)}, u32[]{:S(2)}) copy-start(bf16[2,5120]{1,0:T(2,128)(2,1)} %param.6) | copy-start | bytes 61444
  356.3 282.3 %copy-start.1 = (f32[5120]{0:T(1024)S(1)}, f32[5120]{0:T(1024)}, u32[]{:S(2)}) copy-start(f32[5120]{0:T(1024)} %param.7) | copy-start | bytes 61444
Sparse Core Ops, SparseCore 0:
  356.4 282.1 all-reduce.4
